TPU v7x, 32 devices: a whole 2x2x4 slice. The times are simulated.
32 devices in a mesh: rows: 8 (over y, x, core), cols: 4 (over z).
Axes of the slice: x: 2, y: 2, z: 4, core: 2. Of those that a mesh axis runs over, the one named last changes fastest.
Arguments:
- features: bfloat16 [64, 256, 512], P('rows', 'cols'), may hold values from -6 to 6
- w_l2l: bfloat16 [3, 3, 128, 128], replicated, may hold values from -0.09375 to 0.09375
- w_g2l: bfloat16 [3, 3, 384, 128], replicated, may hold values from -0.09375 to 0.09375
- w_l2g: bfloat16 [3, 3, 128, 384], replicated, may hold values from -0.1875 to 0.1875
- w_in: bfloat16 [384, 192], replicated, may hold values from -0.3125 to 0.3125
- in_scale: float32 [192], replicated, may hold values from 0.5 to 1.5
- in_shift: float32 [192], replicated, may hold values from -2.5 to 2.5
- w_fu: bfloat16 [384, 384], replicated, may hold values from -0.3125 to 0.3125
- fu_scale: float32 [384], replicated, may hold values from 0.1 to 1.9
- fu_shift: float32 [384], replicated, may hold values from -2.5 to 2.5
- w_out: bfloat16 [192, 384], replicated, may hold values from -0.4375 to 0.4375
- local_scale: float32 [128], replicated, may hold values from 0.5 to 1.5
- local_shift: float32 [128], replicated, may hold values from -2.5 to 2.5
- global_scale: float32 [384], replicated, may hold values from 0.5 to 1.5
- global_shift: float32 [384], replicated, may hold values from -2.5 to 2.5
Outputs:
- out_local: bfloat16 [64, 256, 128], P('rows', 'cols')
- out_global: bfloat16 [64, 256, 384], P('rows', 'cols')
All inputs are finite; a program needn't handle non-finite values.
Results may differ from a plain program's by a relative error of at most 0.0085.
Values may be sent and summed in bfloat16 or wider, within the bound.
A program may use at most 64 MiB of HBM per device.

v0:
```python
import math

import jax
import jax.numpy as jnp
from jax import lax
from jax.sharding import PartitionSpec as P


def padded_2(x, sides, width):
    for axis, dim in sides:
        size, length = (lax.axis_size(axis), x.shape[dim])
        up = [(i, (i + 1) % size) for i in range(size - 1)]
        down = [(j, i) for i, j in up]
        last = lax.slice_in_dim(x, length - width, length, axis=dim)
        initial = lax.slice_in_dim(x, 0, width, axis=dim)
        before = lax.ppermute(last, axis, up)
        after = lax.ppermute(initial, axis, down)
        x = jnp.concatenate([before, x, after], axis=dim)
    return x


def rounded(value):
    return lax.optimization_barrier(value.astype(jnp.bfloat16))


def mirror_rows(value):
    return jnp.roll(jnp.flip(value, 0), 1, 0)


def angle_grid(count_a, count_b, modulus):
    left_index = lax.broadcasted_iota(jnp.int32, (count_a, count_b), 0)
    right_index = lax.broadcasted_iota(jnp.int32, (count_a, count_b), 1)
    return (left_index * right_index % modulus).astype(jnp.float32) * (2.0 * math.pi / modulus)


def along_rows(stacked, spectral, direction):
    highest = lax.Precision.HIGHEST
    length = stacked.shape[0]
    angles = angle_grid(length, length, length)
    factor = 1.0 / math.sqrt(length)
    cos_part = jnp.einsum("qh,hkc->qkc", jnp.cos(angles), stacked, precision=highest)
    sin_part = jnp.einsum("qh,hkc->qkc", jnp.sin(angles), stacked, precision=highest)
    if direction < 0:
        out_real = cos_part[..., :spectral] + sin_part[..., spectral:]
        out_imag = cos_part[..., spectral:] - sin_part[..., :spectral]
    else:
        out_real = cos_part[..., :spectral] - sin_part[..., spectral:]
        out_imag = cos_part[..., spectral:] + sin_part[..., :spectral]
    return (out_real * factor, out_imag * factor)


def shards(
    features,
    w_l2l,
    w_g2l,
    w_l2g,
    w_in,
    in_scale,
    in_shift,
    w_fu,
    fu_scale,
    fu_shift,
    w_out,
    local_scale,
    local_shift,
    global_scale,
    global_shift,
):
    floating = jnp.float32
    highest = lax.Precision.HIGHEST
    rows_here, cols_here, channels = features.shape
    local_width = w_l2l.shape[2]
    global_width = w_l2g.shape[3]
    spectral = w_in.shape[1]
    row_count = lax.axis_size("rows")
    col_count = lax.axis_size("cols")
    row_slab = rows_here // col_count
    column_total = cols_here * col_count
    half_width = column_total // 2
    row_total = rows_here * row_count
    per_device = half_width // (row_count * col_count)
    width_factor = 1.0 / math.sqrt(column_total)
    padded = padded_2(features, (("rows", 0), ("cols", 1)), 1)
    at_top = lax.axis_index("rows") == 0
    at_bottom = lax.axis_index("rows") == row_count - 1
    at_left = lax.axis_index("cols") == 0
    at_right = lax.axis_index("cols") == col_count - 1
    is_first = jnp.logical_and(at_top, at_left)
    padded = padded.at[0].set(jnp.where(at_top, padded[2], padded[0]))
    padded = padded.at[-1].set(jnp.where(at_bottom, padded[-3], padded[-1]))
    padded = padded.at[:, 0].set(jnp.where(at_left, padded[:, 2], padded[:, 0]))
    padded = padded.at[:, -1].set(jnp.where(at_right, padded[:, -3], padded[:, -1]))
    projected = jnp.einsum(
        "hwi,io->hwo", features[..., local_width:], w_in, preferred_element_type=floating
    )
    reduced = rounded(jnp.maximum(projected * in_scale + in_shift, 0.0))
    spread = lax.all_to_all(
        reduced.reshape(col_count, row_slab, cols_here, spectral),
        "cols",
        split_axis=0,
        concat_axis=2,
        tiled=True,
    )
    spread = spread.reshape(row_slab, column_total, spectral)
    pixel_index = lax.broadcasted_iota(jnp.int32, (column_total, half_width), 0)
    freq_index = lax.broadcasted_iota(jnp.int32, (column_total, half_width), 1)
    alternate = jnp.where(pixel_index % 2 == 0, 1.0, -1.0).astype(floating)
    forward_angles = angle_grid(column_total, half_width, column_total)
    forward_cos = jnp.cos(forward_angles)
    forward_sin = jnp.where(freq_index == 0, alternate, -jnp.sin(forward_angles))
    spread_float = spread.astype(floating)
    width_real = (
        jnp.einsum("hwc,wk->hkc", spread_float, forward_cos, precision=highest) * width_factor
    )
    width_imag = (
        jnp.einsum("hwc,wk->hkc", spread_float, forward_sin, precision=highest) * width_factor
    )
    width_spec = jnp.concatenate([width_real, width_imag], axis=-1).astype(jnp.bfloat16)
    width_spec = width_spec.reshape(1, row_slab, row_count, col_count, per_device, 2 * spectral)
    gathered = lax.all_to_all(
        lax.all_to_all(width_spec, "rows", split_axis=2, concat_axis=0, tiled=True),
        "cols",
        split_axis=3,
        concat_axis=1,
        tiled=True,
    )
    w_local = jnp.concatenate([w_l2l, w_g2l], axis=2)
    local_total = jnp.zeros((rows_here * cols_here, local_width), floating)
    cross_total = jnp.zeros((rows_here * cols_here, global_width), floating)
    for row_step in range(3):
        for col_step in range(3):
            window = padded[
                row_step : row_step + rows_here, col_step : col_step + cols_here
            ].reshape(-1, channels)
            local_total = local_total + jnp.dot(
                window, w_local[row_step, col_step], preferred_element_type=floating
            )
            cross_total = cross_total + jnp.dot(
                window[:, :local_width], w_l2g[row_step, col_step], preferred_element_type=floating
            )
    out_local = jnp.maximum(local_total * local_scale + local_shift, 0.0).astype(jnp.bfloat16)
    out_local = out_local.reshape(rows_here, cols_here, local_width)
    columns = gathered.reshape(row_total, per_device, 2 * spectral).astype(floating)
    spec_real, spec_imag = along_rows(columns, spectral, -1.0)
    spec_real = rounded(spec_real)
    spec_imag = rounded(spec_imag)
    first_real = spec_real[:, 0].astype(floating)
    first_imag = spec_imag[:, 0].astype(floating)
    mirror_real = mirror_rows(first_real)
    mirror_imag = mirror_rows(first_imag)
    zero_real = rounded((first_real + mirror_real) * 0.5)
    zero_imag = rounded((first_imag - mirror_imag) * 0.5)
    top_real = rounded((first_imag + mirror_imag) * 0.5)
    top_imag = rounded((mirror_real - first_real) * 0.5)
    lead_real = jnp.where(is_first, zero_real, spec_real[:, 0])
    lead_imag = jnp.where(is_first, zero_imag, spec_imag[:, 0])
    all_real = jnp.concatenate([lead_real[:, None], spec_real[:, 1:], top_real[:, None]], axis=1)
    all_imag = jnp.concatenate([lead_imag[:, None], spec_imag[:, 1:], top_imag[:, None]], axis=1)
    cells = jnp.concatenate([all_real, all_imag], axis=-1).reshape(
        row_total * (per_device + 1), 2 * spectral
    )
    reorder = jnp.concatenate([jnp.arange(spectral) * 2, jnp.arange(spectral) * 2 + 1])
    w_mix = w_fu[reorder][:, reorder]
    mixed_cells = rounded(
        jnp.maximum(
            jnp.dot(cells, w_mix, preferred_element_type=floating) * fu_scale[reorder]
            + fu_shift[reorder],
            0.0,
        )
    )
    mixed_grid = mixed_cells.reshape(row_total, per_device + 1, 2 * spectral).astype(floating)
    low_real = mixed_grid[:, 0, :spectral]
    low_imag = mixed_grid[:, 0, spectral:]
    high_real = mixed_grid[:, per_device, :spectral]
    high_imag = mixed_grid[:, per_device, spectral:]
    joint_real = (low_real + mirror_rows(low_real) - high_imag + mirror_rows(high_imag)) * 0.5
    joint_imag = (low_imag - mirror_rows(low_imag) + high_real + mirror_rows(high_real)) * 0.5
    joint = jnp.concatenate([joint_real, joint_imag], axis=-1)
    lead = jnp.where(is_first, joint, mixed_grid[:, 0])
    into = jnp.concatenate([lead[:, None], mixed_grid[:, 1:per_device]], axis=1)
    back_real, back_imag = along_rows(into, spectral, 1.0)
    back_rows = jnp.concatenate([back_real, back_imag], axis=-1).astype(jnp.bfloat16)
    back_rows = back_rows.reshape(row_total, 1, 1, per_device, 2 * spectral)
    returned = lax.all_to_all(
        lax.all_to_all(back_rows, "rows", split_axis=0, concat_axis=1, tiled=True),
        "cols",
        split_axis=0,
        concat_axis=2,
        tiled=True,
    )
    rows_grid = returned.reshape(row_slab, half_width, 2 * spectral).astype(floating)
    back_freq = lax.broadcasted_iota(jnp.int32, (half_width, column_total), 0)
    back_pixel = lax.broadcasted_iota(jnp.int32, (half_width, column_total), 1)
    back_alternate = jnp.where(back_pixel % 2 == 0, 1.0, -1.0).astype(floating)
    back_angles = angle_grid(half_width, column_total, column_total)
    back_cos = jnp.where(back_freq == 0, 1.0, 2.0 * jnp.cos(back_angles))
    back_sin = jnp.where(back_freq == 0, -back_alternate, 2.0 * jnp.sin(back_angles))
    fourier_real = jnp.einsum("hkc,kw->hwc", rows_grid[..., :spectral], back_cos, precision=highest)
    fourier_real = fourier_real - jnp.einsum(
        "hkc,kw->hwc", rows_grid[..., spectral:], back_sin, precision=highest
    )
    fourier = rounded(fourier_real * width_factor)
    joined = rounded(spread.astype(floating) + fourier.astype(floating))
    terms = jnp.einsum("hwc,co->hwo", joined, w_out, preferred_element_type=floating)
    terms = terms.reshape(row_slab, col_count, cols_here, global_width)
    projection = (
        lax.all_to_all(terms.astype(jnp.bfloat16), "cols", split_axis=1, concat_axis=0, tiled=True)
        .astype(terms.dtype)
        .reshape(rows_here, cols_here, global_width)
    )
    global_sum = cross_total.reshape(rows_here, cols_here, global_width) + projection
    out_global = jnp.maximum(global_sum * global_scale + global_shift, 0.0).astype(jnp.bfloat16)
    return (out_local, out_global)


def solution(mesh):
    placed = (
        P("rows", "cols", None),
        P(),
        P(),
        P(),
        P(),
        P(),
        P(),
        P(),
        P(),
        P(),
        P(),
        P(),
        P(),
        P(),
        P(),
    )
    return jax.shard_map(
        shards,
        mesh=mesh,
        in_specs=placed,
        out_specs=(P("rows", "cols", None), P("rows", "cols", None)),
        check_vma=False,
    )
```

profile of v0, /device:TPU:0, one launch (start us, length us, event | category | flops | bytes accessed | tf_op | source)
XLA Modules:
  0.0 139.5 jit_solution(15899544166050075286)
XLA Ops:
  1.6 2.5 %collective-permute-start = (bf16[1,64,512]{2,1,0:T(8,128)(2,1)S(1)}, bf16[1,64,512]{2,1,0:T(8,128)(2,1)S(1)}, u32[]{:S(2)}, u32[]{:S(2)}) collective-permute-start(bf16[1,64,512]{2,1,0:T(8,128)(2,1)S(1)} %get-tuple-element.78), channel_id=1, source_target_pairs={{0,4},{4,8},{8,12},{12,16},{16,20},{20,24},{24,28},{1,5},{5,9},{9,... | collective-permute-start | bytes 196616 | tf_op jit(solution)/shard_map/ppermute | solution.py:16
  5.4 2.1 %fusion.4 = bf16[8,64,192]{2,1,0:T(8,128)(2,1)} fusion(bf16[8,64,512]{2,1,0:T(8,128)(2,1)} %param.23, f32[192]{0:T(256)} %param.29, f32[192]{0:T(256)} %param.28, bf16[384,192]{0,1:T(8,128)(2,1)} %param.27), kind=kOutput, calls=%fused_computation.19 | convolution fusion | flops 75890688 | bytes 739328 | tf_op jit(solution)/shard_map/hwi,io->hwo/dot_general | solution.py:93
  7.5 5.7 %all-to-all-start = ((bf16[4,2,64,192]{3,2,1,0:T(8,128)(2,1)}), bf16[4,2,64,192]{3,2,1,0:T(8,128)(2,1)S(1)}, u32[]{:S(2)}, u32[]{:S(2)}) async-start(bf16[4,2,64,192]{3,2,1,0:T(8,128)(2,1)} %bitcast.30), calls=%async_computation | async-start | bytes 524288 | tf_op jit(solution)/shard_map/all_to_all | solution.py:97
  16.8 4.5 %collective-permute-start.2 = (bf16[10,1,512]{2,1,0:T(2,128)(2,1)S(1)}, bf16[10,1,512]{2,1,0:T(2,128)(2,1)S(1)}, u32[]{:S(2)}, u32[]{:S(2)}) collective-permute-start(bf16[10,1,512]{2,1,0:T(2,128)(2,1)S(1)} %get-tuple-element.75), channel_id=1, source_target_pairs={{0,1},{1,2},{2,3},{4,5},{5,6},{6,7},{8,9},{9,10},{10,11},{12,13},{... | collective-permute-start | bytes 30728 | tf_op jit(solution)/shard_map/ppermute | solution.py:16
  21.4 2.1 %gather_fusion = bf16[384,384]{1,0:T(8,128)(2,1)S(1)} fusion(bf16[384,384]{1,0:T(8,128)(2,1)S(1)} %copy-done, s32[1024]{0:T(1024)S(1)} %pad_clamp_fusion), kind=kCustom, calls=%fused_computation | custom fusion | bytes 591360 | tf_op jit(solution)/shard_map/gather | solution.py:163
  23.7 2.5 %gather_fusion.1 = bf16[384,384]{1,0:T(8,128)(2,1)} fusion(bf16[384,384]{0,1:T(8,128)(2,1)S(1)} %copy.159, s32[1024]{0:T(1024)S(1)} %pad_clamp_fusion), kind=kCustom, calls=%fused_computation.1 | custom fusion | bytes 591360 | tf_op jit(solution)/shard_map/gather | solution.py:163
  26.3 2.8 %gather_fusion.3 = f32[384]{0:T(512)S(1)} fusion(f32[384]{0:T(512)S(1)} %copy-done.1, s32[1024]{0:T(1024)S(1)} %pad_clamp_fusion), kind=kCustom, calls=%fused_computation.3 | custom fusion | bytes 4608 | tf_op jit(solution)/shard_map/gather | solution.py:167
  29.1 2.8 %gather_fusion.2 = f32[384]{0:T(512)S(1)} fusion(f32[384]{0:T(512)S(1)} %copy-done.2, s32[1024]{0:T(1024)S(1)} %pad_clamp_fusion), kind=kCustom, calls=%fused_computation.2 | custom fusion | bytes 4608 | tf_op jit(solution)/shard_map/gather | solution.py:166
  42.6 2.4 %fusion.58 = f32[128,384]{0,1} fusion(bf16[256,384]{0,1:T(8,128)(2,1)} %bitcast.245), kind=kOutput, calls=%fused_computation.114 | convolution fusion | flops 151453696 | bytes 393216
  49.3 2.0 %maximum_bitcast_fusion = bf16[1,2,8,4,4,384]{5,1,4,3,0,2:T(2,128)(2,1)} fusion(bf16[1,2,8,4,4,192]{5,1,4,3,2,0:T(2,128)(2,1)} %bitcast.248, bf16[1,2,8,4,4,192]{5,1,4,3,2,0:T(2,128)(2,1)} %bitcast.249), kind=kLoop, calls=%fused_computation.60 | loop fusion | flops 393216 | bytes 393216 | tf_op jit(solution)/shard_map/concatenate | solution.py:118
  51.3 6.3 %all-to-all-start.1 = ((bf16[1,2,8,4,4,384]{5,1,4,3,0,2:T(2,128)(2,1)}), bf16[1,2,8,4,4,384]{5,1,4,3,0,2:T(2,128)(2,1)}, u32[]{:S(2)}, u32[]{:S(2)}) async-start(bf16[1,2,8,4,4,384]{5,1,4,3,0,2:T(2,128)(2,1)} %maximum_bitcast_fusion), calls=%async_computation.1 | async-start | bytes 393216 | tf_op jit(solution)/shard_map/all_to_all | solution.py:121
  57.5 2.1 %convolution_add_fusion.12 = f32[512,128]{1,0:T(8,128)} fusion(f32[512,128]{1,0:T(8,128)S(1)} %copy-done.11, bf16[512,512]{1,0:T(8,128)(2,1)} %bitcast.232, bf16[3,3,512,128]{3,2,1,0:T(8,128)(2,1)} %constant_dynamic-update-slice_fusion.3), kind=kOutput, calls=%fused_computation.25 | convolution fusion | flops 67174400 | bytes 1179648 | tf_op jit(solution)/shard_map/dot_general | solution.py:135
  59.6 4.3 %all-to-all-done.1 = bf16[1,2,8,4,4,384]{5,1,4,3,0,2:T(2,128)(2,1)} async-done(((bf16[1,2,8,4,4,384]{5,1,4,3,0,2:T(2,128)(2,1)}), bf16[1,2,8,4,4,384]{5,1,4,3,0,2:T(2,128)(2,1)}, u32[]{:S(2)}, u32[]{:S(2)}) %all-to-all-start.1) | async-done | bytes 196640 | tf_op jit(solution)/shard_map/all_to_all | solution.py:121
  65.6 4.2 %all-to-all-start.2 = ((bf16[8,2,1,4,4,384]{5,1,4,0,2,3:T(2,128)(2,1)}), bf16[8,2,1,4,4,384]{5,1,4,0,2,3:T(2,128)(2,1)}, u32[]{:S(2)}, u32[]{:S(2)}) async-start(bf16[8,2,1,4,4,384]{5,1,4,0,2,3:T(2,128)(2,1)} %copy.156), calls=%async_computation.2 | async-start | bytes 393216 | tf_op jit(solution)/shard_map/all_to_all | solution.py:120
  69.8 2.0 %convolution_add_fusion.11 = f32[512,128]{1,0:T(8,128)} fusion(f32[512,128]{1,0:T(8,128)} %convolution_add_fusion.12, bf16[512,512]{1,0:T(8,128)(2,1)S(1)} %bitcast.229, bf16[3,3,512,128]{3,2,1,0:T(8,128)(2,1)} %constant_dynamic-update-slice_fusion.3), kind=kOutput, calls=%fused_computation.24 | convolution fusion | flops 67174400 | bytes 1179648 | tf_op jit(solution)/shard_map/dot_general | solution.py:135
  73.1 4.5 %all-to-all-done.2 = bf16[8,2,1,4,4,384]{5,1,4,0,2,3:T(2,128)(2,1)} async-done(((bf16[8,2,1,4,4,384]{5,1,4,0,2,3:T(2,128)(2,1)}), bf16[8,2,1,4,4,384]{5,1,4,0,2,3:T(2,128)(2,1)}, u32[]{:S(2)}, u32[]{:S(2)}) %all-to-all-start.2) | async-done | bytes 196640 | tf_op jit(solution)/shard_map/all_to_all | solution.py:120
  85.9 2.0 %fusion.5 = bf16[320,384]{1,0:T(8,128)(2,1)} fusion(bf16[320,384]{1,0:T(8,128)(2,1)S(1)} %reshape.343, bf16[384,384]{1,0:T(8,128)(2,1)} %gather_fusion.1, f32[384]{0:T(512)S(1)} %gather_fusion.3, f32[384]{0:T(512)S(1)} %gather_fusion.2), kind=kOutput, calls=%fused_computation.20 | convolution fusion | flops 94863360 | bytes 789504 | tf_op jit(solution)/shard_map/dot_general | solution.py:166
  98.3 3.4 %all-to-all-start.3 = ((bf16[64,1,1,4,384]{4,3,2,1,0:T(4,128)(2,1)}), bf16[64,1,1,4,384]{4,3,2,1,0:T(4,128)(2,1)S(1)}, u32[]{:S(2)}, u32[]{:S(2)}) async-start(bf16[64,1,1,4,384]{4,3,2,1,0:T(4,128)(2,1)} %copy.174), calls=%async_computation.3 | async-start | bytes 393216 | tf_op jit(solution)/shard_map/all_to_all | solution.py:185
  102.9 5.0 %all-to-all-done.3 = bf16[64,1,1,4,384]{4,3,2,1,0:T(4,128)(2,1)S(1)} async-done(((bf16[64,1,1,4,384]{4,3,2,1,0:T(4,128)(2,1)}), bf16[64,1,1,4,384]{4,3,2,1,0:T(4,128)(2,1)S(1)}, u32[]{:S(2)}, u32[]{:S(2)}) %all-to-all-start.3) | async-done | bytes 196640 | tf_op jit(solution)/shard_map/all_to_all | solution.py:185
  108.6 4.0 %all-to-all-start.4 = ((bf16[8,8,1,4,384]{4,1,3,2,0:T(8,128)(2,1)}), bf16[8,8,1,4,384]{4,1,3,2,0:T(8,128)(2,1)}, u32[]{:S(2)}, u32[]{:S(2)}) async-start(bf16[8,8,1,4,384]{4,1,3,2,0:T(8,128)(2,1)} %copy.176), calls=%async_computation.4 | async-start | bytes 393216 | tf_op jit(solution)/shard_map/all_to_all | solution.py:184
  112.6 1.9 %convolution_add_fusion.9 = f32[512,128]{1,0:T(8,128)} fusion(f32[512,128]{1,0:T(8,128)S(1)} %convolution_add_fusion.10, bf16[512,512]{1,0:T(8,128)(2,1)S(1)} %bitcast.225, bf16[3,3,512,128]{3,2,1,0:T(8,128)(2,1)} %constant_dynamic-update-slice_fusion.3), kind=kOutput, calls=%fused_computation.22 | convolution fusion | flops 67174400 | bytes 1179648 | tf_op jit(solution)/shard_map/dot_general | solution.py:135
  115.7 4.4 %all-to-all-done.4 = bf16[8,8,1,4,384]{4,1,3,2,0:T(8,128)(2,1)} async-done(((bf16[8,8,1,4,384]{4,1,3,2,0:T(8,128)(2,1)}), bf16[8,8,1,4,384]{4,1,3,2,0:T(8,128)(2,1)}, u32[]{:S(2)}, u32[]{:S(2)}) %all-to-all-start.4) | async-done | bytes 196640 | tf_op jit(solution)/shard_map/all_to_all | solution.py:184
  124.7 3.5 %all-to-all-start.5 = ((bf16[2,4,64,384]{3,2,0,1:T(8,128)(2,1)}), bf16[2,4,64,384]{3,2,0,1:T(8,128)(2,1)S(1)}, u32[]{:S(2)}, u32[]{:S(2)}) async-start(bf16[2,4,64,384]{3,2,0,1:T(8,128)(2,1)} %copy.180), calls=%async_computation.5 | async-start | bytes 786432 | tf_op jit(solution)/shard_map/all_to_all | solution.py:207
  132.4 6.1 %all-to-all-done.5 = bf16[2,4,64,384]{3,2,0,1:T(8,128)(2,1)S(1)} async-done(((bf16[2,4,64,384]{3,2,0,1:T(8,128)(2,1)}), bf16[2,4,64,384]{3,2,0,1:T(8,128)(2,1)S(1)}, u32[]{:S(2)}, u32[]{:S(2)}) %all-to-all-start.5) | async-done | bytes 393248 | tf_op jit(solution)/shard_map/all_to_all | solution.py:207
  (173 shorter events, 54.7 us)
Async XLA Ops:
  0.6 20.7 %copy-start = (bf16[384,384]{1,0:T(8,128)(2,1)S(1)}, bf16[384,384]{1,0:T(8,128)(2,1)}, u32[]{:S(2)}) copy-start(bf16[384,384]{1,0:T(8,128)(2,1)} %param.30) | copy-start | bytes 884740
  0.6 12.6 %copy-start.18 = (bf16[3,3,128,128]{3,2,1,0:T(8,128)(2,1)S(1)}, bf16[3,3,128,128]{3,2,1,0:T(8,128)(2,1)}, u32[]{:S(2)}) copy-start(bf16[3,3,128,128]{3,2,1,0:T(8,128)(2,1)} %param.24) | copy-start | bytes 884740
  1.6 12.6 %copy-start.13 = (bf16[3,3,384,128]{3,2,1,0:T(8,128)(2,1)S(1)}, bf16[3,3,384,128]{3,2,1,0:T(8,128)(2,1)}, u32[]{:S(2)}) copy-start(bf16[3,3,384,128]{3,2,1,0:T(8,128)(2,1)} %param.25) | copy-start | bytes 2654212
  1.6 13.7 %collective-permute-start = (bf16[1,64,512]{2,1,0:T(8,128)(2,1)S(1)}, bf16[1,64,512]{2,1,0:T(8,128)(2,1)S(1)}, u32[]{:S(2)}, u32[]{:S(2)}) collective-permute-start(bf16[1,64,512]{2,1,0:T(8,128)(2,1)S(1)} %get-tuple-element.78), channel_id=1, source_target_pairs={{0,4},{4,8},{8,12},{12,16},{16,20},{20,24},{24,28},{1,5},{5,9},{9,... | collective-permute-start | bytes 196616 | tf_op jit(solution)/shard_map/ppermute | solution.py:16
  4.1 11.3 %collective-permute-start.1 = (bf16[1,64,512]{2,1,0:T(8,128)(2,1)S(1)}, bf16[1,64,512]{2,1,0:T(8,128)(2,1)S(1)}, u32[]{:S(2)}, u32[]{:S(2)}) collective-permute-start(bf16[1,64,512]{2,1,0:T(8,128)(2,1)S(1)} %get-tuple-element.77), channel_id=1, source_target_pairs={{4,0},{8,4},{12,8},{16,12},{20,16},{24,20},{28,24},{5,1},{9,5},{13... | collective-permute-start | bytes 196616 | tf_op jit(solution)/shard_map/ppermute | solution.py:17
  7.5 32.5 %all-to-all-start = ((bf16[4,2,64,192]{3,2,1,0:T(8,128)(2,1)}), bf16[4,2,64,192]{3,2,1,0:T(8,128)(2,1)S(1)}, u32[]{:S(2)}, u32[]{:S(2)}) async-start(bf16[4,2,64,192]{3,2,1,0:T(8,128)(2,1)} %bitcast.30), calls=%async_computation | async-start | bytes 524288 | tf_op jit(solution)/shard_map/all_to_all | solution.py:97
  15.3 29.7 %copy-start.25 = (pred[256]{0:T(512)(128)(4,1)}, pred[256]{0:T(512)(128)(4,1)S(1)}, u32[]{:S(2)}) copy-start(pred[256]{0:T(512)(128)(4,1)S(1)} %compare_and_fusion) | copy-start | bytes 772
  15.5 16.4 %collective-permute-start.3 = (bf16[10,1,512]{2,1,0:T(2,128)(2,1)S(1)}, bf16[10,1,512]{2,1,0:T(2,128)(2,1)S(1)}, u32[]{:S(2)}, u32[]{:S(2)}) collective-permute-start(bf16[10,1,512]{2,1,0:T(2,128)(2,1)S(1)} %get-tuple-element.76), channel_id=1, source_target_pairs={{1,0},{2,1},{3,2},{5,4},{6,5},{7,6},{9,8},{10,9},{11,10},{13,12},{... | collective-permute-start | bytes 30728 | tf_op jit(solution)/shard_map/ppermute | solution.py:17
  16.8 15.2 %collective-permute-start.2 = (bf16[10,1,512]{2,1,0:T(2,128)(2,1)S(1)}, bf16[10,1,512]{2,1,0:T(2,128)(2,1)S(1)}, u32[]{:S(2)}, u32[]{:S(2)}) collective-permute-start(bf16[10,1,512]{2,1,0:T(2,128)(2,1)S(1)} %get-tuple-element.75), channel_id=1, source_target_pairs={{0,1},{1,2},{2,3},{4,5},{5,6},{6,7},{8,9},{9,10},{10,11},{12,13},{... | collective-permute-start | bytes 30728 | tf_op jit(solution)/shard_map/ppermute | solution.py:16
  21.3 23.7 %copy-start.27 = (pred[128]{0:T(512)(128)(4,1)}, pred[128]{0:T(512)(128)(4,1)S(1)}, u32[]{:S(2)}) copy-start(pred[128]{0:T(512)(128)(4,1)S(1)} %iota_compare_fusion) | copy-start | bytes 388
  33.1 6.7 %copy-start.5 = (bf16[8,64,512]{2,1,0:T(8,128)(2,1)}, bf16[8,64,512]{2,1,0:T(8,128)(2,1)S(1)}, u32[]{:S(2)}) copy-start(bf16[8,64,512]{2,1,0:T(8,128)(2,1)S(1)} %get-tuple-element.70) | copy-start | bytes 1572868
  33.1 36.7 %copy-start.4 = (bf16[8,64,512]{2,1,0:T(8,128)(2,1)}, bf16[8,64,512]{2,1,0:T(8,128)(2,1)S(1)}, u32[]{:S(2)}) copy-start(bf16[8,64,512]{2,1,0:T(8,128)(2,1)S(1)} %get-tuple-element.69) | copy-start | bytes 1572868
  46.8 10.8 %copy-start.11 = (f32[512,128]{1,0:T(8,128)S(1)}, f32[512,128]{1,0:T(8,128)}, u32[]{:S(2)}) copy-start(f32[512,128]{1,0:T(8,128)} %convolution_add_fusion.13) | copy-start | bytes 786436
  51.3 12.6 %all-to-all-start.1 = ((bf16[1,2,8,4,4,384]{5,1,4,3,0,2:T(2,128)(2,1)}), bf16[1,2,8,4,4,384]{5,1,4,3,0,2:T(2,128)(2,1)}, u32[]{:S(2)}, u32[]{:S(2)}) async-start(bf16[1,2,8,4,4,384]{5,1,4,3,0,2:T(2,128)(2,1)} %maximum_bitcast_fusion), calls=%async_computation.1 | async-start | bytes 393216 | tf_op jit(solution)/shard_map/all_to_all | solution.py:121
  65.6 12.0 %all-to-all-start.2 = ((bf16[8,2,1,4,4,384]{5,1,4,0,2,3:T(2,128)(2,1)}), bf16[8,2,1,4,4,384]{5,1,4,0,2,3:T(2,128)(2,1)}, u32[]{:S(2)}, u32[]{:S(2)}) async-start(bf16[8,2,1,4,4,384]{5,1,4,0,2,3:T(2,128)(2,1)} %copy.156), calls=%async_computation.2 | async-start | bytes 393216 | tf_op jit(solution)/shard_map/all_to_all | solution.py:120
  98.3 9.6 %all-to-all-start.3 = ((bf16[64,1,1,4,384]{4,3,2,1,0:T(4,128)(2,1)}), bf16[64,1,1,4,384]{4,3,2,1,0:T(4,128)(2,1)S(1)}, u32[]{:S(2)}, u32[]{:S(2)}) async-start(bf16[64,1,1,4,384]{4,3,2,1,0:T(4,128)(2,1)} %copy.174), calls=%async_computation.3 | async-start | bytes 393216 | tf_op jit(solution)/shard_map/all_to_all | solution.py:185
  108.6 11.5 %all-to-all-start.4 = ((bf16[8,8,1,4,384]{4,1,3,2,0:T(8,128)(2,1)}), bf16[8,8,1,4,384]{4,1,3,2,0:T(8,128)(2,1)}, u32[]{:S(2)}, u32[]{:S(2)}) async-start(bf16[8,8,1,4,384]{4,1,3,2,0:T(8,128)(2,1)} %copy.176), calls=%async_computation.4 | async-start | bytes 393216 | tf_op jit(solution)/shard_map/all_to_all | solution.py:184
  114.5 7.0 %copy-start.28 = (pred[128]{0:T(512)(128)(4,1)S(1)}, pred[128]{0:T(512)(128)(4,1)}, u32[]{:S(2)}) copy-start(pred[128]{0:T(512)(128)(4,1)} %copy-done.27) | copy-start | bytes 388
  115.7 6.9 %copy-start.26 = (pred[256]{0:T(512)(128)(4,1)S(1)}, pred[256]{0:T(512)(128)(4,1)}, u32[]{:S(2)}) copy-start(pred[256]{0:T(512)(128)(4,1)} %copy-done.25) | copy-start | bytes 772
  123.6 4.6 %copy-start.9 = (f32[512,128]{1,0:T(8,128)S(1)}, f32[512,128]{1,0:T(8,128)}, u32[]{:S(2)}) copy-start(f32[512,128]{1,0:T(8,128)} %convolution_add_fusion.9) | copy-start | bytes 786436
  123.6 4.6 %copy-start.23 = (f32[128]{0:T(128)S(1)}, f32[128]{0:T(128)}, u32[]{:S(2)}) copy-start(f32[128]{0:T(128)} %param.35) | copy-start | bytes 1540
  124.7 13.8 %all-to-all-start.5 = ((bf16[2,4,64,384]{3,2,0,1:T(8,128)(2,1)}), bf16[2,4,64,384]{3,2,0,1:T(8,128)(2,1)S(1)}, u32[]{:S(2)}, u32[]{:S(2)}) async-start(bf16[2,4,64,384]{3,2,0,1:T(8,128)(2,1)} %copy.180), calls=%async_computation.5 | async-start | bytes 786432 | tf_op jit(solution)/shard_map/all_to_all | solution.py:207
  131.2 7.4 %copy-start.21 = (f32[384]{0:T(512)S(1)}, f32[384]{0:T(512)}, u32[]{:S(2)}) copy-start(f32[384]{0:T(512)} %param.37) | copy-start | bytes 4612
  131.2 7.4 %copy-start.22 = (f32[384]{0:T(512)S(1)}, f32[384]{0:T(512)}, u32[]{:S(2)}) copy-start(f32[384]{0:T(512)} %param.36) | copy-start | bytes 4612
  (16 other events, 38.0 us)
where the time goes:
time: 141 us; the launch traced here: 140 us
  starting transfers between devices  36.6 us (26%)
  matrix products  33.9 us (24%)
  local copies, waits for them, and re-layouts  33.8 us (24%)
  waiting for transfers between devices  24.3 us (17%)
  other arithmetic  9.25 us (7%)
  between operations  1.63 us (1%)
    dot_general x9, matrix products, shards(): jnp.dot(window, w_local[row_step, col_step], preferred_element_type=float...  14.8 us
    ppermute x2, starting transfers between devices, padded_2(): before = lax.ppermute(last, axis, up)  7.04 us
    unnamed x69, local copies, waits for them, and re-layouts  6.62 us
    all_to_all x1, starting transfers between devices, shards(): lax.all_to_all(width_spec, 'rows', split_axis=2, concat_axis=0, tiled=True)  6.25 us
    all_to_all x1, waiting for transfers between devices, shards(): lax.all_to_all(terms.astype(jnp.bfloat16), 'cols', split_axis=1, concat_a...  6.13 us
    unnamed x4, matrix products  5.85 us
    dot_general x9, matrix products, shards(): jnp.dot(window[:, :local_width], w_l2g[row_step, col_step], preferred_ele...  5.82 us
    all_to_all x1, starting transfers between devices, shards(): lax.all_to_all(reduced.reshape(col_count, row_slab, cols_here, spectral),...  5.7 us
  transfers between devices with their start and end apart: 10, of which 5 were waited for; matrix products, arithmetic and copies ran while one was open for 26% of the time, Pallas kernels for 0%

commit v1 on v0

--- a/solution.py
+++ b/solution.py
@@ -1,9 +1,16 @@
+import functools
 import math
 
 import jax
 import jax.numpy as jnp
+import ml_dtypes
+import numpy as np
 from jax import lax
+from jax.experimental import pallas as pl
+from jax.experimental.pallas import tpu as pltpu
 from jax.sharding import PartitionSpec as P
+
+MESH = pl.DeviceIdType.MESH
 
 
 def padded_2(x, sides, width):
@@ -213,6 +220,412 @@
     return (out_local, out_global)
 
 
+def tables(rows, cols, height, width, pad_k):
+    count = rows * cols
+    cell = width // count
+    half = width // 2
+    freq = np.arange(count)[:, None]
+    line = np.arange(height)[None, :]
+    turn = 2.0 * np.pi * ((freq * line) % height) / height
+    row_cos = np.cos(turn)
+    row_sin = -np.sin(turn)
+    row_sin[0] = 1.0 - 2.0 * (np.arange(height) % 2)
+    by_row = np.stack([row_cos, row_sin], 1) / math.sqrt(height)
+    row_forward = np.einsum("qph,wv->qpwhv", by_row, np.eye(cell))
+    row_forward = row_forward.reshape(2 * count * cell, height * cell)
+
+    device = np.arange(count)
+    start = (width // cols) * (device % cols) + cell * (device // cols)
+    column = start[:, None] + np.arange(cell)[None, :]
+    wave = np.arange(half + 1)
+    angle = 2.0 * np.pi * ((wave[:, None, None] * column[None]) % width) / width
+    cosine = np.cos(angle)
+    sine = np.sin(angle)
+    sine[0] = 0.0
+    sine[half] = 0.0
+    weight = np.where((wave == 0) | (wave == half), 1.0, 2.0)[:, None, None]
+    factor = 1.0 / math.sqrt(width)
+    forward = np.zeros((2, 2, 2, pad_k, count, 2, cell))
+    inverse = np.zeros((2, count, 2, cell, 2, 2, pad_k))
+    used = slice(0, half + 1)
+    forward[0, 0, 0, used, :, 0] = cosine
+    forward[0, 1, 0, used, :, 0] = -sine
+    forward[0, 0, 1, used, :, 1] = cosine
+    forward[0, 1, 1, used, :, 1] = -sine
+    for chosen, sign in ((0, 1.0), (1, -1.0)):
+        forward[1, 0, chosen, used, :, 0] = cosine
+        forward[1, 0, chosen, used, :, 1] = sign * sine
+        forward[1, 1, chosen, used, :, 0] = -sine
+        forward[1, 1, chosen, used, :, 1] = sign * cosine
+    back_cos = np.moveaxis(weight * cosine, 0, -1)
+    back_sin = np.moveaxis(weight * sine, 0, -1)
+    inverse[0, :, 0, :, 0, 0, used] = back_cos
+    inverse[0, :, 0, :, 1, 0, used] = -back_sin
+    inverse[0, :, 1, :, 0, 1, used] = back_cos
+    inverse[0, :, 1, :, 1, 1, used] = -back_sin
+    for chosen, sign in ((0, 1.0), (1, -1.0)):
+        inverse[1, :, 0, :, 0, chosen, used] = back_cos
+        inverse[1, :, 0, :, 1, chosen, used] = -back_sin
+        inverse[1, :, 1, :, 0, chosen, used] = sign * back_sin
+        inverse[1, :, 1, :, 1, chosen, used] = sign * back_cos
+    forward = (forward * factor).reshape(2, 4 * pad_k, 2 * count * cell)
+    inverse = (inverse * factor).reshape(2, 2 * count * cell, 4 * pad_k)
+    narrow = ml_dtypes.bfloat16
+    return (
+        row_forward.astype(narrow),
+        np.ascontiguousarray(row_forward.T).astype(narrow),
+        forward.astype(narrow),
+        inverse.astype(narrow),
+    )
+
+
+def mm(left, right):
+    return jnp.dot(left, right, preferred_element_type=jnp.float32)
+
+
+def kernel(
+    rows, cols,
+    feat_h, l2l_h, g2l_h, l2g_h, win_h, wfu_h, wout_h, rowf_h, rowi_h, colf_h, coli_h,
+    in_scale, in_shift, fu_scale, fu_shift, loc_scale, loc_shift, glo_scale, glo_shift,
+    outl_h, outg_h,
+    pad, l2l, g2l, l2g, win, wfu, wout, rowf, rowi, colf, coli,
+    mixers, norms, send_a, recv_a, send_b, recv_b, send_c, recv_c, send_d, recv_d,
+    edge_out, edge_in, near, wide, acc_local, acc_cross, outl, outg,
+    load_sem, sa, ra, sb, rb, sc, rc, sd, rd, sh, rh, store_sem,
+):
+    f32, b16 = jnp.float32, jnp.bfloat16
+    count = rows * cols
+    row = lax.axis_index("rows")
+    col = lax.axis_index("cols")
+    me = row * cols + col
+    tall, across = pad.shape[0] - 2, pad.shape[1]
+    local = l2l.shape[2]
+    spec = win.shape[1]
+    cell = across // rows
+    channels = pad.shape[2]
+    pixels = tall * across
+
+    barrier = pltpu.get_barrier_semaphore()
+
+    def greet(i, carry):
+        j = lax.rem(me + i, count)
+        pl.semaphore_signal(
+            barrier, inc=1, device_id=(j // cols, lax.rem(j, cols)), device_id_type=MESH
+        )
+        return carry
+
+    variant = jnp.where(me == 0, 0, 1)
+    loads = [
+        pltpu.make_async_copy(source, target, load_sem.at[i])
+        for i, (source, target) in enumerate(
+            [
+                (feat_h, pad.at[pl.ds(1, tall)]),
+                (win_h, win),
+                (rowf_h, rowf),
+                (wfu_h, wfu),
+                (colf_h.at[variant], colf),
+                (coli_h.at[variant], coli),
+                (rowi_h, rowi),
+                (l2l_h, l2l),
+                (g2l_h, g2l),
+                (l2g_h, l2g),
+                (wout_h, wout),
+            ]
+        )
+    ]
+    for load in loads:
+        load.start()
+    lax.fori_loop(1, count, greet, 0)
+
+    loads[0].wait()
+    loads[1].wait()
+    inner = pad[1 : tall + 1, :, local:].reshape(pixels, channels - local)
+    reduced = jnp.maximum(mm(inner, win[...]) * in_scale[...] + in_shift[...], 0.0)
+    reduced = reduced.reshape(tall, across, spec)
+    for j in range(rows):
+        block = reduced[:, j * cell : (j + 1) * cell, :].reshape(tall * cell, spec)
+        send_a[j] = block.astype(b16)
+    pl.semaphore_wait(barrier, count - 1)
+
+    def in_column(source, target, sent, got):
+        def begin(i, carry):
+            j = lax.rem(row + i, rows)
+            pltpu.make_async_remote_copy(
+                src_ref=source.at[j], dst_ref=target.at[row], send_sem=sent.at[j],
+                recv_sem=got.at[row], device_id=(j, col), device_id_type=MESH,
+            ).start()
+            return carry
+
+        lax.fori_loop(1, rows, begin, 0)
+        target[row] = source[row]
+
+    def in_column_wait(source, target, sent, got):
+        def end(i, carry):
+            j = lax.rem(row + i, rows)
+            pltpu.make_async_remote_copy(
+                src_ref=source.at[j], dst_ref=target.at[j], send_sem=sent.at[j],
+                recv_sem=got.at[j], device_id=(j, col), device_id_type=MESH,
+            ).wait()
+            return carry
+
+        lax.fori_loop(1, rows, end, 0)
+
+    def everywhere(source, target, sent, got):
+        def begin(i, carry):
+            j = lax.rem(me + i, count)
+            pltpu.make_async_remote_copy(
+                src_ref=source.at[j], dst_ref=target.at[me], send_sem=sent.at[j],
+                recv_sem=got.at[me], device_id=(j // cols, lax.rem(j, cols)),
+                device_id_type=MESH,
+            ).start()
+            return carry
+
+        lax.fori_loop(1, count, begin, 0)
+        target[me] = source[me]
+
+    def everywhere_wait(source, target, sent, got):
+        def end(i, carry):
+            j = lax.rem(me + i, count)
+            pltpu.make_async_remote_copy(
+                src_ref=source.at[j], dst_ref=target.at[j], send_sem=sent.at[j],
+                recv_sem=got.at[j], device_id=(j // cols, lax.rem(j, cols)),
+                device_id_type=MESH,
+            ).wait()
+            return carry
+
+        lax.fori_loop(1, count, end, 0)
+
+    in_column(send_a, recv_a, sa, ra)
+
+    up, down = lax.rem(row + rows - 1, rows), lax.rem(row + 1, rows)
+    left, right = lax.rem(col + cols - 1, cols), lax.rem(col + 1, cols)
+    halo = [
+        pltpu.make_async_remote_copy(
+            src_ref=source, dst_ref=target, send_sem=sh.at[i], recv_sem=rh.at[i],
+            device_id=place, device_id_type=MESH,
+        )
+        for i, (source, target, place) in enumerate(
+            [
+                (pad.at[1], pad.at[tall + 1], (up, col)),
+                (pad.at[tall], pad.at[0], (down, col)),
+                (edge_out.at[0], edge_in.at[1], (row, left)),
+                (edge_out.at[1], edge_in.at[0], (row, right)),
+            ]
+        )
+    ]
+    halo[0].start()
+    halo[1].start()
+
+    loads[3].wait()
+    both = 2 * spec
+    for part_in in range(2):
+        pick_row = (
+            lax.broadcasted_iota(jnp.int32, (spec, both), 1)
+            == 2 * lax.broadcasted_iota(jnp.int32, (spec, both), 0) + part_in
+        )
+        picked = mm(pick_row.astype(f32).astype(b16), wfu[...]).astype(b16)
+        for part_out in range(2):
+            pick_col = (
+                lax.broadcasted_iota(jnp.int32, (both, spec), 0)
+                == 2 * lax.broadcasted_iota(jnp.int32, (both, spec), 1) + part_out
+            ).astype(f32)
+            mixers[part_in, part_out] = mm(picked, pick_col.astype(b16)).astype(b16)
+            if part_in == 0:
+                pair = jnp.concatenate(
+                    [
+                        jnp.broadcast_to(fu_scale[...], (8, both)),
+                        jnp.broadcast_to(fu_shift[...], (8, both)),
+                    ],
+                    axis=0,
+                )
+                norms[part_out] = jnp.dot(
+                    pair, pick_col, precision=lax.Precision.HIGHEST, preferred_element_type=f32
+                )
+
+    loads[2].wait()
+    in_column_wait(send_a, recv_a, sa, ra)
+    spread = mm(rowf[...], recv_a[...].reshape(pixels, spec))
+    send_b[...] = spread.astype(b16).reshape(send_b.shape)
+    everywhere(send_b, recv_b, sb, rb)
+
+    halo[0].wait()
+    halo[1].wait()
+
+    @pl.when(row == 0)
+    def _():
+        pad[0] = pad[2]
+
+    @pl.when(row == rows - 1)
+    def _():
+        pad[tall + 1] = pad[tall - 1]
+
+    edge_rows = edge_out.shape[1]
+    place = lax.broadcasted_iota(jnp.int32, (edge_rows, channels), 0)
+    columns = [jnp.zeros((edge_rows, channels), f32) for _ in range(4)]
+    for p in range(tall + 2):
+        first = pad[p, :16, :].astype(f32)
+        last = pad[p, across - 16 :, :].astype(f32)
+        found = (first[0:1], last[15:16], first[1:2], last[14:15])
+        columns = [jnp.where(place == p, f, c) for f, c in zip(found, columns)]
+    edge_out[0] = columns[0].astype(b16)
+    edge_out[1] = columns[1].astype(b16)
+    halo[2].start()
+    halo[3].start()
+    halo[2].wait()
+    halo[3].wait()
+    before = jnp.where(col == 0, columns[2], edge_in[0].astype(f32))
+    after = jnp.where(col == cols - 1, columns[3], edge_in[1].astype(f32))
+    spot = lax.broadcasted_iota(jnp.int32, (across, channels), 0)
+    wide_channels = channels - local
+    for p in range(tall + 2):
+        here = pad[p].astype(f32)
+        shifted = (
+            jnp.where(spot == 0, before[p : p + 1], pltpu.roll(here, 1, 0)).astype(b16),
+            pad[p],
+            jnp.where(spot == across - 1, after[p : p + 1], pltpu.roll(here, across - 1, 0)).astype(
+                b16
+            ),
+        )
+        span = slice(p * across, (p + 1) * across)
+        for s, value in enumerate(shifted):
+            near[span, s * local : (s + 1) * local] = value[:, :local]
+            wide[span, s * wide_channels : (s + 1) * wide_channels] = value[:, local:]
+
+    def convolve(dy):
+        span = slice(dy * across, dy * across + pixels)
+        close = near[span]
+        local_part = mm(close, l2l[dy]) + mm(wide[span], g2l[dy])
+        cross_part = mm(close, l2g[dy])
+        if dy == 0:
+            acc_local[...] = local_part
+            acc_cross[...] = cross_part
+        else:
+            acc_local[...] += local_part
+            acc_cross[...] += cross_part
+
+    for i in (7, 8, 9):
+        loads[i].wait()
+    convolve(0)
+
+    loads[4].wait()
+    loads[5].wait()
+    everywhere_wait(send_b, recv_b, sb, rb)
+    cells = mm(colf[...], recv_b[...].reshape(pixels, spec)).astype(b16)
+    middle = cells.shape[0] // 2
+    cells_real, cells_imag = cells[:middle], cells[middle:]
+    mixed = []
+    for part in range(2):
+        total = mm(cells_real, mixers[0, part]) + mm(cells_imag, mixers[1, part])
+        mixed.append(
+            jnp.maximum(total * norms[part, 0:1, :] + norms[part, 8:9, :], 0.0).astype(b16)
+        )
+    returned = mm(coli[...], jnp.concatenate(mixed, axis=0))
+    send_c[...] = returned.astype(b16).reshape(send_c.shape)
+    everywhere(send_c, recv_c, sc, rc)
+
+    convolve(1)
+    loads[6].wait()
+    everywhere_wait(send_c, recv_c, sc, rc)
+    image = mm(rowi[...], recv_c[...].reshape(pixels, spec))
+    send_d[...] = image.astype(b16).reshape(send_d.shape)
+    in_column(send_d, recv_d, sd, rd)
+
+    convolve(2)
+    local_out = jnp.maximum(acc_local[...] * loc_scale[...] + loc_shift[...], 0.0)
+    outl[...] = local_out.astype(b16).reshape(outl.shape)
+    store_local = pltpu.make_async_copy(outl, outl_h, store_sem.at[0])
+    store_local.start()
+
+    loads[10].wait()
+    in_column_wait(send_d, recv_d, sd, rd)
+    blocks = [send_a[j].astype(f32) + recv_d[j].astype(f32) for j in range(rows)]
+    joined = jnp.concatenate(
+        [blocks[j][h * cell : (h + 1) * cell] for h in range(tall) for j in range(rows)], axis=0
+    ).astype(b16)
+    total = acc_cross[...] + mm(joined, wout[...])
+    global_out = jnp.maximum(total * glo_scale[...] + glo_shift[...], 0.0)
+    outg[...] = global_out.astype(b16).reshape(outg.shape)
+    store_global = pltpu.make_async_copy(outg, outg_h, store_sem.at[1])
+    store_global.start()
+    store_local.wait()
+    store_global.wait()
+
+
+def fused(rows, cols, features, *rest):
+    (
+        w_l2l, w_g2l, w_l2g, w_in, in_scale, in_shift, w_fu, fu_scale, fu_shift, w_out,
+        local_scale, local_shift, global_scale, global_shift,
+    ) = rest
+    tall, across, channels = features.shape
+    count = rows * cols
+    height, width = tall * rows, across * cols
+    if tall != 8 or height != 2 * count or width != 8 * count or across != 8 * rows:
+        return shards(features, *rest)
+    b16, f32 = jnp.bfloat16, jnp.float32
+    local, glob, spec = w_l2l.shape[2], w_l2g.shape[3], w_in.shape[1]
+    pixels = tall * across
+    cell = across // rows
+    pad_k = -(-(width // 2 + 1) // 16) * 16
+    table = [jnp.asarray(t) for t in tables(rows, cols, height, width, pad_k)]
+    weights = [
+        w_l2l.reshape(3, 3 * w_l2l.shape[2], local),
+        w_g2l.reshape(3, 3 * w_g2l.shape[2], local),
+        w_l2g.reshape(3, 3 * w_l2g.shape[2], glob),
+        w_in, w_fu, w_out,
+    ]
+    vectors = [
+        v.reshape(1, -1)
+        for v in (
+            in_scale, in_shift, fu_scale, fu_shift, local_scale, local_shift, global_scale,
+            global_shift,
+        )
+    ]
+    anywhere = pl.BlockSpec(memory_space=pl.ANY)
+    inside = pl.BlockSpec(memory_space=pltpu.VMEM)
+    V = pltpu.VMEM
+    many = pltpu.SemaphoreType.DMA
+    by_row = V((rows, tall * cell, spec), b16)
+    by_device = V((count, 2 * cell, spec), b16)
+    return pl.pallas_call(
+        functools.partial(kernel, rows, cols),
+        out_shape=(
+            jax.ShapeDtypeStruct((tall, across, local), b16),
+            jax.ShapeDtypeStruct((tall, across, glob), b16),
+        ),
+        in_specs=[anywhere] * 11 + [inside] * 8,
+        out_specs=(anywhere, anywhere),
+        scratch_shapes=[
+            V((tall + 2, across, channels), b16),
+            *[V(w.shape, b16) for w in weights],
+            V(table[0].shape, b16),
+            V(table[1].shape, b16),
+            V(table[2].shape[1:], b16),
+            V(table[3].shape[1:], b16),
+            V((2, 2, spec, spec), b16),
+            V((2, 16, spec), f32),
+            by_row, by_row, by_device, by_device, by_device, by_device, by_row, by_row,
+            V((2, 16, channels), b16),
+            V((2, 16, channels), b16),
+            V(((tall + 2) * across, 3 * local), b16),
+            V(((tall + 2) * across, 3 * (channels - local)), b16),
+            V((pixels, local), f32),
+            V((pixels, glob), f32),
+            V((tall, across, local), b16),
+            V((tall, across, glob), b16),
+            many((11,)),
+            many((rows,)), many((rows,)),
+            many((count,)), many((count,)),
+            many((count,)), many((count,)),
+            many((rows,)), many((rows,)),
+            many((4,)), many((4,)),
+            many((2,)),
+        ],
+        compiler_params=pltpu.CompilerParams(
+            collective_id=0, has_side_effects=True, vmem_limit_bytes=56 * 1024 * 1024
+        ),
+    )(features, *weights, *table, *vectors)
+
+
 def solution(mesh):
     placed = (
         P("rows", "cols", None),
@@ -232,7 +645,7 @@
         P(),
     )
     return jax.shard_map(
-        shards,
+        functools.partial(fused, mesh.shape["rows"], mesh.shape["cols"]),
         mesh=mesh,
         in_specs=placed,
         out_specs=(P("rows", "cols", None), P("rows", "cols", None)),

time: 141 us -> 50.7 us (0.36)
  Pallas kernels: 0 us -> 39.7 us
  starting transfers between devices: 36.6 us -> 0 us
  matrix products: 33.9 us -> 0 us
  waiting for transfers between devices: 24.3 us -> 0 us
  local copies, waits for them, and re-layouts: 33.8 us -> 10.1 us
  other arithmetic: 9.25 us -> 0 us
    pallas_call x0 -> x1, Pallas kernels: none -> 39.7 us  [fused(): pl.pallas_call(functools.partial(kernel, rows, cols), out_shape=(jax.Shap...]
    dot_general x25 -> x0, matrix products: 28.1 us -> none  [the longest x9 14.8 us: shards(): jnp.dot(window, w_local[row_step, col_step], preferred_element_type=float...]
    all_to_all x6 -> x0, starting transfers between devices: 27 us -> none  [the longest x1 6.25 us: shards(): lax.all_to_all(width_spec, 'rows', split_axis=2, concat_axis=0, tiled=True)]
    all_to_all x6 -> x0, waiting for transfers between devices: 24.3 us -> none  [the longest x1 6.13 us: shards(): lax.all_to_all(terms.astype(jnp.bfloat16), 'cols', split_axis=1, concat_a...]
    gather x5 -> x0, local copies, waits for them, and re-layouts: 10.5 us -> none  [the longest x3 4.89 us: shards(): w_mix = w_fu[reorder][:, reorder]]
    ppermute x4 -> x0, starting transfers between devices: 9.62 us -> none  [the longest x2 7.04 us: padded_2(): before = lax.ppermute(last, axis, up)]
    unnamed x4 -> x0, matrix products: 5.85 us -> none
    all_to_all x6 -> x0, local copies, waits for them, and re-layouts: 5.57 us -> none  [the longest x1 1.74 us: shards(): lax.all_to_all(width_spec, 'rows', split_axis=2, concat_axis=0, tiled=True)]
  transfers between devices with their start and end apart: 10 -> 0, of which waited for: 5 -> 0; matrix products, arithmetic and copies ran while one was open for 26% -> 0% of each run, Pallas kernels for 0% -> 0%
where the time goes in v1:
time: 50.7 us; the launch traced here: 50.4 us
  Pallas kernels  39.7 us (78%)
  local copies, waits for them, and re-layouts  10.1 us (20%)
  between operations  0.64 us (1%)
    pallas_call x1, Pallas kernels, fused(): pl.pallas_call(functools.partial(kernel, rows, cols), out_shape=(jax.Shap...  39.7 us
    unnamed x3, local copies, waits for them, and re-layouts  5.07 us
    reshape x4, local copies, waits for them, and re-layouts, fused(): v.reshape(1, -1)  4.99 us

profile of v1, /device:TPU:0, one launch (start us, length us, event | category | flops | bytes accessed | tf_op | source)
XLA Modules:
  0.0 50.4 jit_solution(13806151594351173830)
XLA Ops:
  0.6 1.2 %reshape.42.fu_scale = f32[1,384]{1,0:T(1,128)} reshape(f32[384]{0:T(512)} %param.27) | data formatting | bytes 3072 | tf_op jit(solution)/shard_map/reshape | solution.py:577
  1.9 1.3 %reshape.43.fu_shift = f32[1,384]{1,0:T(1,128)} reshape(f32[384]{0:T(512)} %param.28) | data formatting | bytes 3072 | tf_op jit(solution)/shard_map/reshape | solution.py:577
  3.1 1.3 %reshape.46.glo_scale = f32[1,384]{1,0:T(1,128)} reshape(f32[384]{0:T(512)} %param.32) | data formatting | bytes 3072 | tf_op jit(solution)/shard_map/reshape | solution.py:577
  4.4 1.2 %reshape.47.glo_shift = f32[1,384]{1,0:T(1,128)} reshape(f32[384]{0:T(512)} %param.33) | data formatting | bytes 3072 | tf_op jit(solution)/shard_map/reshape | solution.py:577
  5.6 1.7 %copy.21.win_h = bf16[384,192]{1,0:T(8,128)(2,1)} copy(bf16[384,192]{0,1:T(8,128)(2,1)} %param.23) | data formatting | bytes 294912 | tf_op args[4]
  7.3 39.7 %shard_map.194 = (bf16[8,64,128]{2,1,0:T(8,128)(2,1)}, bf16[8,64,384]{2,1,0:T(8,128)(2,1)}) custom-call(bf16[8,64,512]{2,1,0:T(8,128)(2,1)} %feat_h.1, bf16[3,384,128]{2,1,0:T(8,128)(2,1)} %bitcast.9, bf16[3,1152,128]{2,1,0:T(8,128)(2,1)} %bitcast.7, bf16[3,384,384]{2,1,0:T(8,128)(2,1)} %bitcast.8, bf16[384,192]{1,0:T(8,128)(2,1)} %copy.21.win_h, ...), custom_call_target="tpu_custom_call" | custom-call | tf_op jit(solution)/shard_map/pallas_call | solution.py:589
  47.1 1.6 %copy.24 = bf16[8,64,128]{2,1,0:T(8,128)(2,1)} copy(bf16[8,64,128]{2,1,0:T(8,128)(2,1)} %get-tuple-element.4) | data formatting | bytes 262144
  48.6 1.8 %copy.25 = bf16[8,64,384]{2,1,0:T(8,128)(2,1)} copy(bf16[8,64,384]{2,1,0:T(8,128)(2,1)} %get-tuple-element.5) | data formatting | bytes 786432

commit v2 on v1

--- a/solution.py
+++ b/solution.py
@@ -283,15 +283,36 @@
     return jnp.dot(left, right, preferred_element_type=jnp.float32)
 
 
+def mm_nt(left, right):
+    return lax.dot_general(
+        left, right, (((1,), (1,)), ((), ())), preferred_element_type=jnp.float32
+    )
+
+
+def line(vector):
+    return vector[...].reshape(1, vector.shape[0])
+
+
+def hand_over(first, second, first_out, second_out, sems):
+    copies = [
+        pltpu.make_async_copy(first, first_out, sems.at[0]),
+        pltpu.make_async_copy(second, second_out, sems.at[1]),
+    ]
+    for copy in copies:
+        copy.start()
+    for copy in copies:
+        copy.wait()
+
+
 def kernel(
     rows, cols,
     feat_h, l2l_h, g2l_h, l2g_h, win_h, wfu_h, wout_h, rowf_h, rowi_h, colf_h, coli_h,
     in_scale, in_shift, fu_scale, fu_shift, loc_scale, loc_shift, glo_scale, glo_shift,
-    outl_h, outg_h,
+    outl, outg,
     pad, l2l, g2l, l2g, win, wfu, wout, rowf, rowi, colf, coli,
     mixers, norms, send_a, recv_a, send_b, recv_b, send_c, recv_c, send_d, recv_d,
-    edge_out, edge_in, near, wide, acc_local, acc_cross, outl, outg,
-    load_sem, sa, ra, sb, rb, sc, rc, sd, rd, sh, rh, store_sem,
+    edge_out, edge_in, near, wide, acc_local, acc_cross,
+    load_sem, sa, ra, sb, rb, sc, rc, sd, rd, sh, rh,
 ):
     f32, b16 = jnp.float32, jnp.bfloat16
     count = rows * cols
@@ -300,7 +321,7 @@
     me = row * cols + col
     tall, across = pad.shape[0] - 2, pad.shape[1]
     local = l2l.shape[2]
-    spec = win.shape[1]
+    spec = win.shape[0]
     cell = across // rows
     channels = pad.shape[2]
     pixels = tall * across
@@ -340,7 +361,7 @@
     loads[0].wait()
     loads[1].wait()
     inner = pad[1 : tall + 1, :, local:].reshape(pixels, channels - local)
-    reduced = jnp.maximum(mm(inner, win[...]) * in_scale[...] + in_shift[...], 0.0)
+    reduced = jnp.maximum(mm_nt(inner, win[...]) * line(in_scale) + line(in_shift), 0.0)
     reduced = reduced.reshape(tall, across, spec)
     for j in range(rows):
         block = reduced[:, j * cell : (j + 1) * cell, :].reshape(tall * cell, spec)
@@ -415,6 +436,12 @@
     ]
     halo[0].start()
     halo[1].start()
+
+    loads[2].wait()
+    in_column_wait(send_a, recv_a, sa, ra)
+    spread = mm(rowf[...], recv_a[...].reshape(pixels, spec))
+    send_b[...] = spread.astype(b16).reshape(send_b.shape)
+    everywhere(send_b, recv_b, sb, rb)
 
     loads[3].wait()
     both = 2 * spec
@@ -433,20 +460,14 @@
             if part_in == 0:
                 pair = jnp.concatenate(
                     [
-                        jnp.broadcast_to(fu_scale[...], (8, both)),
-                        jnp.broadcast_to(fu_shift[...], (8, both)),
+                        jnp.broadcast_to(line(fu_scale), (8, both)),
+                        jnp.broadcast_to(line(fu_shift), (8, both)),
                     ],
                     axis=0,
                 )
                 norms[part_out] = jnp.dot(
                     pair, pick_col, precision=lax.Precision.HIGHEST, preferred_element_type=f32
                 )
-
-    loads[2].wait()
-    in_column_wait(send_a, recv_a, sa, ra)
-    spread = mm(rowf[...], recv_a[...].reshape(pixels, spec))
-    send_b[...] = spread.astype(b16).reshape(send_b.shape)
-    everywhere(send_b, recv_b, sb, rb)
 
     halo[0].wait()
     halo[1].wait()
@@ -531,10 +552,8 @@
     in_column(send_d, recv_d, sd, rd)
 
     convolve(2)
-    local_out = jnp.maximum(acc_local[...] * loc_scale[...] + loc_shift[...], 0.0)
+    local_out = jnp.maximum(acc_local[...] * line(loc_scale) + line(loc_shift), 0.0)
     outl[...] = local_out.astype(b16).reshape(outl.shape)
-    store_local = pltpu.make_async_copy(outl, outl_h, store_sem.at[0])
-    store_local.start()
 
     loads[10].wait()
     in_column_wait(send_d, recv_d, sd, rd)
@@ -543,12 +562,8 @@
         [blocks[j][h * cell : (h + 1) * cell] for h in range(tall) for j in range(rows)], axis=0
     ).astype(b16)
     total = acc_cross[...] + mm(joined, wout[...])
-    global_out = jnp.maximum(total * glo_scale[...] + glo_shift[...], 0.0)
+    global_out = jnp.maximum(total * line(glo_scale) + line(glo_shift), 0.0)
     outg[...] = global_out.astype(b16).reshape(outg.shape)
-    store_global = pltpu.make_async_copy(outg, outg_h, store_sem.at[1])
-    store_global.start()
-    store_local.wait()
-    store_global.wait()
 
 
 def fused(rows, cols, features, *rest):
@@ -571,14 +586,11 @@
         w_l2l.reshape(3, 3 * w_l2l.shape[2], local),
         w_g2l.reshape(3, 3 * w_g2l.shape[2], local),
         w_l2g.reshape(3, 3 * w_l2g.shape[2], glob),
-        w_in, w_fu, w_out,
+        w_in.T, w_fu, w_out,
     ]
     vectors = [
-        v.reshape(1, -1)
-        for v in (
-            in_scale, in_shift, fu_scale, fu_shift, local_scale, local_shift, global_scale,
-            global_shift,
-        )
+        in_scale, in_shift, fu_scale, fu_shift, local_scale, local_shift, global_scale,
+        global_shift,
     ]
     anywhere = pl.BlockSpec(memory_space=pl.ANY)
     inside = pl.BlockSpec(memory_space=pltpu.VMEM)
@@ -586,14 +598,12 @@
     many = pltpu.SemaphoreType.DMA
     by_row = V((rows, tall * cell, spec), b16)
     by_device = V((count, 2 * cell, spec), b16)
-    return pl.pallas_call(
+    shapes = ((tall, across, local), (tall, across, glob))
+    made = pl.pallas_call(
         functools.partial(kernel, rows, cols),
-        out_shape=(
-            jax.ShapeDtypeStruct((tall, across, local), b16),
-            jax.ShapeDtypeStruct((tall, across, glob), b16),
-        ),
+        out_shape=tuple(V(shape, b16) for shape in shapes),
         in_specs=[anywhere] * 11 + [inside] * 8,
-        out_specs=(anywhere, anywhere),
+        out_specs=(inside, inside),
         scratch_shapes=[
             V((tall + 2, across, channels), b16),
             *[V(w.shape, b16) for w in weights],
@@ -610,20 +620,24 @@
             V(((tall + 2) * across, 3 * (channels - local)), b16),
             V((pixels, local), f32),
             V((pixels, glob), f32),
-            V((tall, across, local), b16),
-            V((tall, across, glob), b16),
             many((11,)),
             many((rows,)), many((rows,)),
             many((count,)), many((count,)),
             many((count,)), many((count,)),
             many((rows,)), many((rows,)),
             many((4,)), many((4,)),
-            many((2,)),
         ],
         compiler_params=pltpu.CompilerParams(
             collective_id=0, has_side_effects=True, vmem_limit_bytes=56 * 1024 * 1024
         ),
     )(features, *weights, *table, *vectors)
+    return pl.pallas_call(
+        hand_over,
+        out_shape=tuple(jax.ShapeDtypeStruct(shape, b16) for shape in shapes),
+        in_specs=[inside, inside],
+        out_specs=(anywhere, anywhere),
+        scratch_shapes=[many((2,))],
+    )(*made)
 
 
 def solution(mesh):

time: 50.7 us -> 43.1 us (0.85)
  local copies, waits for them, and re-layouts: 10.1 us -> 1.4 us
  Pallas kernels: 39.7 us -> 40.9 us
    reshape x4 -> x0, local copies, waits for them, and re-layouts: 4.99 us -> none  [fused(): v.reshape(1, -1)]
    unnamed x3 -> x4, local copies, waits for them, and re-layouts: 5.07 us -> 1.4 us
    pallas_call x1 -> x2, Pallas kernels: 39.7 us -> 40.9 us  [the longest x1 39 us: fused(): pl.pallas_call(functools.partial(kernel, rows, cols), out_shape=tuple((V(...]
where the time goes in v2:
time: 43.1 us; the launch traced here: 42.9 us
  Pallas kernels  40.9 us (95%)
  local copies, waits for them, and re-layouts  1.4 us (3%)
  between operations  0.65 us (2%)
    pallas_call x1, Pallas kernels, fused(): pl.pallas_call(functools.partial(kernel, rows, cols), out_shape=tuple((V(...  39 us
    pallas_call x1, Pallas kernels, fused(): pl.pallas_call(hand_over, out_shape=tuple((jax.ShapeDtypeStruct(shape, b1...  1.87 us
    unnamed x4, local copies, waits for them, and re-layouts  1.4 us

profile of v2, /device:TPU:0, one launch (start us, length us, event | category | flops | bytes accessed | tf_op | source)
XLA Modules:
  0.0 42.9 jit_solution(17446299172369524494)
XLA Ops:
  0.6 39.0 %shard_map.194 = (bf16[8,64,128]{2,1,0:T(8,128)(2,1)S(1)}, bf16[8,64,384]{2,1,0:T(8,128)(2,1)S(1)}) custom-call(bf16[8,64,512]{2,1,0:T(8,128)(2,1)} %feat_h.1, bf16[3,384,128]{2,1,0:T(8,128)(2,1)} %bitcast.6, bf16[3,1152,128]{2,1,0:T(8,128)(2,1)} %bitcast.4, bf16[3,384,384]{2,1,0:T(8,128)(2,1)} %bitcast.5, bf16[192,384]{1,0:T(8,128)(2,1)} %bitcast.7, ...), custom_call_target="tpu_custom_call" | custom-call | tf_op jit(solution)/shard_map/pallas_call | solution.py:602
  39.6 0.0 copy-start
  39.7 0.7 %copy-done = bf16[8,64,384]{2,1,0:T(8,128)(2,1)} copy-done((bf16[8,64,384]{2,1,0:T(8,128)(2,1)}, bf16[8,64,384]{2,1,0:T(8,128)(2,1)S(1)}, u32[]{:S(2)}) %copy-start) | copy-done | bytes 393240
  40.4 0.0 copy-start.1
  40.4 0.7 %copy-done.1 = bf16[8,64,128]{2,1,0:T(8,128)(2,1)} copy-done((bf16[8,64,128]{2,1,0:T(8,128)(2,1)}, bf16[8,64,128]{2,1,0:T(8,128)(2,1)S(1)}, u32[]{:S(2)}) %copy-start.1) | copy-done | bytes 131096
  41.1 1.9 %shard_map.195 = (bf16[8,64,128]{2,1,0:T(8,128)(2,1)}, bf16[8,64,384]{2,1,0:T(8,128)(2,1)}) custom-call(bf16[8,64,128]{2,1,0:T(8,128)(2,1)} %copy-done.1, bf16[8,64,384]{2,1,0:T(8,128)(2,1)} %copy-done), custom_call_target="tpu_custom_call" | custom-call | tf_op jit(solution)/shard_map/pallas_call | solution.py:634
Async XLA Ops:
  39.6 0.8 %copy-start = (bf16[8,64,384]{2,1,0:T(8,128)(2,1)}, bf16[8,64,384]{2,1,0:T(8,128)(2,1)S(1)}, u32[]{:S(2)}) copy-start(bf16[8,64,384]{2,1,0:T(8,128)(2,1)S(1)} %get-tuple-element.5.second) | copy-start | bytes 1179652
  40.4 0.7 %copy-start.1 = (bf16[8,64,128]{2,1,0:T(8,128)(2,1)}, bf16[8,64,128]{2,1,0:T(8,128)(2,1)S(1)}, u32[]{:S(2)}) copy-start(bf16[8,64,128]{2,1,0:T(8,128)(2,1)S(1)} %get-tuple-element.4.first) | copy-start | bytes 393220

commit v3 on v2

--- a/solution.py
+++ b/solution.py
@@ -289,6 +289,28 @@
     )
 
 
+def packed(value, groups):
+    rows, wide = value.shape
+    base = wide // 128 * 128
+    half = rows // groups // 2
+    low = value[:, :base].reshape(groups, 2 * half, base)
+    high = value[:, base:].reshape(groups, 2, half, wide - base)
+    high = jnp.concatenate([high[:, 0], high[:, 1]], axis=-1)
+    return jnp.concatenate([low, high], axis=1).astype(jnp.bfloat16)
+
+
+def unpacked(value):
+    groups, rows, lanes = value.shape
+    half = rows // 3
+    low = value[:, : 2 * half].reshape(groups * 2 * half, lanes)
+    high = value[:, 2 * half :].reshape(groups * half, lanes)
+    turned = pltpu.roll(high, lanes // 2, 1)
+    high = jnp.concatenate(
+        [high.reshape(groups, 1, half, lanes), turned.reshape(groups, 1, half, lanes)], axis=1
+    ).reshape(groups * 2 * half, lanes)
+    return jnp.concatenate([low, high[:, : lanes // 2]], axis=1)
+
+
 def line(vector):
     return vector[...].reshape(1, vector.shape[0])
 
@@ -354,7 +376,7 @@
             ]
         )
     ]
-    for load in loads:
+    for load in loads[:3]:
         load.start()
     lax.fori_loop(1, count, greet, 0)
 
@@ -363,9 +385,12 @@
     inner = pad[1 : tall + 1, :, local:].reshape(pixels, channels - local)
     reduced = jnp.maximum(mm_nt(inner, win[...]) * line(in_scale) + line(in_shift), 0.0)
     reduced = reduced.reshape(tall, across, spec)
-    for j in range(rows):
-        block = reduced[:, j * cell : (j + 1) * cell, :].reshape(tall * cell, spec)
-        send_a[j] = block.astype(b16)
+    by_block = [
+        reduced[:, j * cell : (j + 1) * cell, :].reshape(tall * cell, spec) for j in range(rows)
+    ]
+    send_a[...] = packed(jnp.concatenate(by_block, axis=0), rows)
+    for load in loads[3:]:
+        load.start()
     pl.semaphore_wait(barrier, count - 1)
 
     def in_column(source, target, sent, got):
@@ -439,8 +464,8 @@
 
     loads[2].wait()
     in_column_wait(send_a, recv_a, sa, ra)
-    spread = mm(rowf[...], recv_a[...].reshape(pixels, spec))
-    send_b[...] = spread.astype(b16).reshape(send_b.shape)
+    spread = mm(rowf[...], unpacked(recv_a[...].astype(f32)).astype(b16))
+    send_b[...] = packed(spread, count)
     everywhere(send_b, recv_b, sb, rb)
 
     loads[3].wait()
@@ -531,7 +556,7 @@
     loads[4].wait()
     loads[5].wait()
     everywhere_wait(send_b, recv_b, sb, rb)
-    cells = mm(colf[...], recv_b[...].reshape(pixels, spec)).astype(b16)
+    cells = mm(colf[...], unpacked(recv_b[...].astype(f32)).astype(b16)).astype(b16)
     middle = cells.shape[0] // 2
     cells_real, cells_imag = cells[:middle], cells[middle:]
     mixed = []
@@ -541,14 +566,14 @@
             jnp.maximum(total * norms[part, 0:1, :] + norms[part, 8:9, :], 0.0).astype(b16)
         )
     returned = mm(coli[...], jnp.concatenate(mixed, axis=0))
-    send_c[...] = returned.astype(b16).reshape(send_c.shape)
+    send_c[...] = packed(returned, count)
     everywhere(send_c, recv_c, sc, rc)
 
     convolve(1)
     loads[6].wait()
     everywhere_wait(send_c, recv_c, sc, rc)
-    image = mm(rowi[...], recv_c[...].reshape(pixels, spec))
-    send_d[...] = image.astype(b16).reshape(send_d.shape)
+    image = mm(rowi[...], unpacked(recv_c[...].astype(f32)).astype(b16))
+    send_d[...] = packed(image, rows)
     in_column(send_d, recv_d, sd, rd)
 
     convolve(2)
@@ -557,7 +582,8 @@
 
     loads[10].wait()
     in_column_wait(send_d, recv_d, sd, rd)
-    blocks = [send_a[j].astype(f32) + recv_d[j].astype(f32) for j in range(rows)]
+    added = unpacked(send_a[...].astype(f32) + recv_d[...].astype(f32))
+    blocks = [added[j * tall * cell : (j + 1) * tall * cell] for j in range(rows)]
     joined = jnp.concatenate(
         [blocks[j][h * cell : (h + 1) * cell] for h in range(tall) for j in range(rows)], axis=0
     ).astype(b16)
@@ -574,7 +600,7 @@
     tall, across, channels = features.shape
     count = rows * cols
     height, width = tall * rows, across * cols
-    if tall != 8 or height != 2 * count or width != 8 * count or across != 8 * rows:
+    if tall != 8 or height != 2 * count or width != 8 * count or across != 8 * rows or w_in.shape[1] != 192:
         return shards(features, *rest)
     b16, f32 = jnp.bfloat16, jnp.float32
     local, glob, spec = w_l2l.shape[2], w_l2g.shape[3], w_in.shape[1]
@@ -596,8 +622,8 @@
     inside = pl.BlockSpec(memory_space=pltpu.VMEM)
     V = pltpu.VMEM
     many = pltpu.SemaphoreType.DMA
-    by_row = V((rows, tall * cell, spec), b16)
-    by_device = V((count, 2 * cell, spec), b16)
+    by_row = V((rows, tall * cell * spec // 128, 128), b16)
+    by_device = V((count, 2 * cell * spec // 128, 128), b16)
     shapes = ((tall, across, local), (tall, across, glob))
     made = pl.pallas_call(
         functools.partial(kernel, rows, cols),
@@ -637,6 +663,7 @@
         in_specs=[inside, inside],
         out_specs=(anywhere, anywhere),
         scratch_shapes=[many((2,))],
+        compiler_params=pltpu.CompilerParams(vmem_limit_bytes=4 * 1024 * 1024),
     )(*made)
 
 

time: 43.1 us -> 37 us (0.86)
  Pallas kernels: 40.9 us -> 36.2 us
  local copies, waits for them, and re-layouts: 1.4 us -> 0 us
    pallas_call x1, Pallas kernels: 39 us -> 35.4 us  [fused(): pl.pallas_call(functools.partial(kernel, rows, cols), out_shape=tuple((V(...]
    unnamed x4 -> x0, local copies, waits for them, and re-layouts: 1.4 us -> none
    pallas_call x1, Pallas kernels: 1.87 us -> 0.81 us  [fused(): pl.pallas_call(hand_over, out_shape=tuple((jax.ShapeDtypeStruct(shape, b1...]
where the time goes in v3:
time: 37 us; the launch traced here: 36.8 us
  Pallas kernels  36.2 us (98%)
  between operations  0.64 us (2%)
    pallas_call x1, Pallas kernels, fused(): pl.pallas_call(functools.partial(kernel, rows, cols), out_shape=tuple((V(...  35.4 us
    pallas_call x1, Pallas kernels, fused(): pl.pallas_call(hand_over, out_shape=tuple((jax.ShapeDtypeStruct(shape, b1...  0.81 us

profile of v3, /device:TPU:0, one launch (start us, length us, event | category | flops | bytes accessed | tf_op | source)
XLA Modules:
  0.0 36.8 jit_solution(234281909709477894)
XLA Ops:
  0.6 35.4 %shard_map.194 = (bf16[8,64,128]{2,1,0:T(8,128)(2,1)S(1)}, bf16[8,64,384]{2,1,0:T(8,128)(2,1)S(1)}) custom-call(bf16[8,64,512]{2,1,0:T(8,128)(2,1)} %feat_h.1, bf16[3,384,128]{2,1,0:T(8,128)(2,1)} %bitcast.6, bf16[3,1152,128]{2,1,0:T(8,128)(2,1)} %bitcast.4, bf16[3,384,384]{2,1,0:T(8,128)(2,1)} %bitcast.5, bf16[192,384]{1,0:T(8,128)(2,1)} %bitcast.7, ...), custom_call_target="tpu_custom_call" | custom-call | tf_op jit(solution)/shard_map/pallas_call | solution.py:628
  36.0 0.8 %shard_map.195 = (bf16[8,64,128]{2,1,0:T(8,128)(2,1)}, bf16[8,64,384]{2,1,0:T(8,128)(2,1)}) custom-call(bf16[8,64,128]{2,1,0:T(8,128)(2,1)S(1)} %get-tuple-element.4.first, bf16[8,64,384]{2,1,0:T(8,128)(2,1)S(1)} %get-tuple-element.5.second), custom_call_target="tpu_custom_call" | custom-call | tf_op jit(solution)/shard_map/pallas_call | solution.py:660

commit v4 on v3

--- a/solution.py
+++ b/solution.py
@@ -350,12 +350,13 @@
 
     barrier = pltpu.get_barrier_semaphore()
 
-    def greet(i, carry):
-        j = lax.rem(me + i, count)
-        pl.semaphore_signal(
-            barrier, inc=1, device_id=(j // cols, lax.rem(j, cols)), device_id_type=MESH
-        )
-        return carry
+    def wrapped(index, size):
+        return jnp.where(index >= size, index - size, index)
+
+    ring = [wrapped(row + i, rows) for i in range(rows)]
+    others = [
+        (ring[a], wrapped(col + b, cols)) for a in range(rows) for b in range(cols) if a or b
+    ]
 
     variant = jnp.where(me == 0, 0, 1)
     loads = [
@@ -378,7 +379,8 @@
     ]
     for load in loads[:3]:
         load.start()
-    lax.fori_loop(1, count, greet, 0)
+    for place in others:
+        pl.semaphore_signal(barrier, inc=1, device_id=place, device_id_type=MESH)
 
     loads[0].wait()
     loads[1].wait()
@@ -393,53 +395,25 @@
         load.start()
     pl.semaphore_wait(barrier, count - 1)
 
+    def push(source, target, sent, got, slot, place, mine):
+        pltpu.make_async_remote_copy(
+            src_ref=source.at[slot], dst_ref=target.at[mine], send_sem=sent.at[0],
+            recv_sem=got.at[0], device_id=place, device_id_type=MESH,
+        ).start()
+
     def in_column(source, target, sent, got):
-        def begin(i, carry):
-            j = lax.rem(row + i, rows)
-            pltpu.make_async_remote_copy(
-                src_ref=source.at[j], dst_ref=target.at[row], send_sem=sent.at[j],
-                recv_sem=got.at[row], device_id=(j, col), device_id_type=MESH,
-            ).start()
-            return carry
-
-        lax.fori_loop(1, rows, begin, 0)
+        for j in ring[1:]:
+            push(source, target, sent, got, j, (j, col), row)
         target[row] = source[row]
 
-    def in_column_wait(source, target, sent, got):
-        def end(i, carry):
-            j = lax.rem(row + i, rows)
-            pltpu.make_async_remote_copy(
-                src_ref=source.at[j], dst_ref=target.at[j], send_sem=sent.at[j],
-                recv_sem=got.at[j], device_id=(j, col), device_id_type=MESH,
-            ).wait()
-            return carry
-
-        lax.fori_loop(1, rows, end, 0)
-
     def everywhere(source, target, sent, got):
-        def begin(i, carry):
-            j = lax.rem(me + i, count)
-            pltpu.make_async_remote_copy(
-                src_ref=source.at[j], dst_ref=target.at[me], send_sem=sent.at[j],
-                recv_sem=got.at[me], device_id=(j // cols, lax.rem(j, cols)),
-                device_id_type=MESH,
-            ).start()
-            return carry
-
-        lax.fori_loop(1, count, begin, 0)
+        for there, beside in others:
+            push(source, target, sent, got, there * cols + beside, (there, beside), me)
         target[me] = source[me]
 
-    def everywhere_wait(source, target, sent, got):
-        def end(i, carry):
-            j = lax.rem(me + i, count)
-            pltpu.make_async_remote_copy(
-                src_ref=source.at[j], dst_ref=target.at[j], send_sem=sent.at[j],
-                recv_sem=got.at[j], device_id=(j // cols, lax.rem(j, cols)),
-                device_id_type=MESH,
-            ).wait()
-            return carry
-
-        lax.fori_loop(1, count, end, 0)
+    def all_of(buffer, sem):
+        part = buffer.at[pl.ds(0, buffer.shape[0] - 1)]
+        pltpu.make_async_copy(part, part, sem.at[0]).wait()
 
     in_column(send_a, recv_a, sa, ra)
 
@@ -463,7 +437,7 @@
     halo[1].start()
 
     loads[2].wait()
-    in_column_wait(send_a, recv_a, sa, ra)
+    all_of(recv_a, ra)
     spread = mm(rowf[...], unpacked(recv_a[...].astype(f32)).astype(b16))
     send_b[...] = packed(spread, count)
     everywhere(send_b, recv_b, sb, rb)
@@ -555,7 +529,7 @@
 
     loads[4].wait()
     loads[5].wait()
-    everywhere_wait(send_b, recv_b, sb, rb)
+    all_of(recv_b, rb)
     cells = mm(colf[...], unpacked(recv_b[...].astype(f32)).astype(b16)).astype(b16)
     middle = cells.shape[0] // 2
     cells_real, cells_imag = cells[:middle], cells[middle:]
@@ -571,7 +545,7 @@
 
     convolve(1)
     loads[6].wait()
-    everywhere_wait(send_c, recv_c, sc, rc)
+    all_of(recv_c, rc)
     image = mm(rowi[...], unpacked(recv_c[...].astype(f32)).astype(b16))
     send_d[...] = packed(image, rows)
     in_column(send_d, recv_d, sd, rd)
@@ -581,7 +555,7 @@
     outl[...] = local_out.astype(b16).reshape(outl.shape)
 
     loads[10].wait()
-    in_column_wait(send_d, recv_d, sd, rd)
+    all_of(recv_d, rd)
     added = unpacked(send_a[...].astype(f32) + recv_d[...].astype(f32))
     blocks = [added[j * tall * cell : (j + 1) * tall * cell] for j in range(rows)]
     joined = jnp.concatenate(
@@ -590,6 +564,8 @@
     total = acc_cross[...] + mm(joined, wout[...])
     global_out = jnp.maximum(total * line(glo_scale) + line(glo_shift), 0.0)
     outg[...] = global_out.astype(b16).reshape(outg.shape)
+    for buffer, sem in ((send_a, sa), (send_b, sb), (send_c, sc), (send_d, sd)):
+        all_of(buffer, sem)
 
 
 def fused(rows, cols, features, *rest):
@@ -647,10 +623,7 @@
             V((pixels, local), f32),
             V((pixels, glob), f32),
             many((11,)),
-            many((rows,)), many((rows,)),
-            many((count,)), many((count,)),
-            many((count,)), many((count,)),
-            many((rows,)), many((rows,)),
+            *[many((1,))] * 8,
             many((4,)), many((4,)),
         ],
         compiler_params=pltpu.CompilerParams(

time: 37 us -> 35.5 us (0.959)
  Pallas kernels: 36.2 us -> 34.7 us
    pallas_call x1, Pallas kernels: 35.4 us -> 33.9 us  [fused(): pl.pallas_call(functools.partial(kernel, rows, cols), out_shape=tuple((V(...]
where the time goes in v4:
time: 35.5 us; the launch traced here: 35.3 us
  Pallas kernels  34.7 us (98%)
  between operations  0.64 us (2%)
    pallas_call x1, Pallas kernels, fused(): pl.pallas_call(functools.partial(kernel, rows, cols), out_shape=tuple((V(...  33.9 us
    pallas_call x1, Pallas kernels, fused(): pl.pallas_call(hand_over, out_shape=tuple((jax.ShapeDtypeStruct(shape, b1...  0.81 us

profile of v4, /device:TPU:0, one launch (start us, length us, event | category | flops | bytes accessed | tf_op | source)
XLA Modules:
  0.0 35.3 jit_solution(11379938393799511245)
XLA Ops:
  0.6 33.9 %shard_map.194 = (bf16[8,64,128]{2,1,0:T(8,128)(2,1)S(1)}, bf16[8,64,384]{2,1,0:T(8,128)(2,1)S(1)}) custom-call(bf16[8,64,512]{2,1,0:T(8,128)(2,1)} %feat_h.1, bf16[3,384,128]{2,1,0:T(8,128)(2,1)} %bitcast.6, bf16[3,1152,128]{2,1,0:T(8,128)(2,1)} %bitcast.4, bf16[3,384,384]{2,1,0:T(8,128)(2,1)} %bitcast.5, bf16[192,384]{1,0:T(8,128)(2,1)} %bitcast.7, ...), custom_call_target="tpu_custom_call" | custom-call | tf_op jit(solution)/shard_map/pallas_call | solution.py:604
  34.5 0.8 %shard_map.195 = (bf16[8,64,128]{2,1,0:T(8,128)(2,1)}, bf16[8,64,384]{2,1,0:T(8,128)(2,1)}) custom-call(bf16[8,64,128]{2,1,0:T(8,128)(2,1)S(1)} %get-tuple-element.4.first, bf16[8,64,384]{2,1,0:T(8,128)(2,1)S(1)} %get-tuple-element.5.second), custom_call_target="tpu_custom_call" | custom-call | tf_op jit(solution)/shard_map/pallas_call | solution.py:633

commit v5 on v4

--- a/solution.py
+++ b/solution.py
@@ -433,14 +433,14 @@
             ]
         )
     ]
-    halo[0].start()
-    halo[1].start()
 
     loads[2].wait()
     all_of(recv_a, ra)
     spread = mm(rowf[...], unpacked(recv_a[...].astype(f32)).astype(b16))
     send_b[...] = packed(spread, count)
     everywhere(send_b, recv_b, sb, rb)
+    halo[0].start()
+    halo[1].start()
 
     loads[3].wait()
     both = 2 * spec

time: 35.5 us -> 36.6 us (1.031)
  Pallas kernels: 34.7 us -> 35.8 us
    pallas_call x1, Pallas kernels: 33.9 us -> 35 us  [fused(): pl.pallas_call(functools.partial(kernel, rows, cols), out_shape=tuple((V(...]
where the time goes in v5:
time: 36.6 us; the launch traced here: 36.5 us
  Pallas kernels  35.8 us (98%)
  between operations  0.64 us (2%)
    pallas_call x1, Pallas kernels, fused(): pl.pallas_call(functools.partial(kernel, rows, cols), out_shape=tuple((V(...  35 us
    pallas_call x1, Pallas kernels, fused(): pl.pallas_call(hand_over, out_shape=tuple((jax.ShapeDtypeStruct(shape, b1...  0.81 us

profile of v5, /device:TPU:0, one launch (start us, length us, event | category | flops | bytes accessed | tf_op | source)
XLA Modules:
  0.0 36.5 jit_solution(5102787982267408990)
XLA Ops:
  0.6 35.0 %shard_map.194 = (bf16[8,64,128]{2,1,0:T(8,128)(2,1)S(1)}, bf16[8,64,384]{2,1,0:T(8,128)(2,1)S(1)}) custom-call(bf16[8,64,512]{2,1,0:T(8,128)(2,1)} %feat_h.1, bf16[3,384,128]{2,1,0:T(8,128)(2,1)} %bitcast.6, bf16[3,1152,128]{2,1,0:T(8,128)(2,1)} %bitcast.4, bf16[3,384,384]{2,1,0:T(8,128)(2,1)} %bitcast.5, bf16[192,384]{1,0:T(8,128)(2,1)} %bitcast.7, ...), custom_call_target="tpu_custom_call" | custom-call | tf_op jit(solution)/shard_map/pallas_call | solution.py:604
  35.6 0.8 %shard_map.195 = (bf16[8,64,128]{2,1,0:T(8,128)(2,1)}, bf16[8,64,384]{2,1,0:T(8,128)(2,1)}) custom-call(bf16[8,64,128]{2,1,0:T(8,128)(2,1)S(1)} %get-tuple-element.4.first, bf16[8,64,384]{2,1,0:T(8,128)(2,1)S(1)} %get-tuple-element.5.second), custom_call_target="tpu_custom_call" | custom-call | tf_op jit(solution)/shard_map/pallas_call | solution.py:633
